TPU v7x, 256 devices: a whole 4x4x8 slice. The times are simulated.
256 devices in a mesh: dp: 32 (over y, z), tensor: 8 (over x, core).
Axes of the slice: x: 4, y: 4, z: 8, core: 2. Of those that a mesh axis runs over, the one named last changes fastest.
Arguments:
- activations: bfloat16 [24576, 5120], P('dp'), may hold values from -6 to 6
- cotangent: bfloat16 [3, 24576, 5120], P(None, 'dp', 'tensor'), may hold values from -0.09375 to 0.09375
- projector: bfloat16 [3, 5120, 512], P(None, 'dp'), may hold values from -0.078125 to 0.078125
- first_moment: float32 [3, 512, 5120], P(None, 'dp', 'tensor'), may hold values from -6 to 6
- second_moment: float32 [3, 512, 5120], P(None, 'dp', 'tensor'), may hold values from 0.3 to 3
Outputs:
- new_first: float32 [3, 512, 5120], P(None, 'dp', 'tensor')
- new_second: float32 [3, 512, 5120], P(None, 'dp', 'tensor')
- update: bfloat16 [3, 5120, 5120], P(None, 'dp', 'tensor')
All inputs are finite; a program needn't handle non-finite values.
Results may differ from a plain program's by a relative error of at most 0.005.
Values may be sent and summed in bfloat16 or wider, within the bound.
A program may use at most 128 MiB of HBM per device.

v0:
```python
import jax
import jax.numpy as jnp
from jax import lax
from jax.sharding import PartitionSpec as P

beta_one = 0.9
beta_two = 0.95
adam_eps = 1e-08
bias_one = 1.0 - 0.9**10
bias_two = 1.0 - 0.95**10


def on_device(activations, cotangent, projector, first_moment, second_moment):
    columns = activations
    lowered = jnp.einsum(
        "tr,krs->kts",
        columns,
        lax.all_gather(projector, "dp", axis=1, tiled=True),
        preferred_element_type=jnp.float32,
    )
    grad_local = jnp.einsum(
        "kts,ktc->ksc", lowered, cotangent.astype(jnp.float32), precision=lax.Precision.HIGHEST
    )
    grad_owned = lax.psum_scatter(grad_local, "dp", scatter_dimension=1, tiled=True)
    fresh_first = beta_one * first_moment + (1.0 - beta_one) * grad_owned
    fresh_second = beta_two * second_moment + (1.0 - beta_two) * grad_owned * grad_owned
    low_step = (fresh_first / bias_one / (jnp.sqrt(fresh_second / bias_two) + adam_eps)).astype(
        jnp.bfloat16
    )
    columns = projector
    expanded = jnp.einsum(
        "krs,ksc->krc",
        columns,
        lax.all_gather(low_step, "dp", axis=1, tiled=True),
        preferred_element_type=jnp.float32,
    )
    return (fresh_first, fresh_second, expanded.astype(jnp.bfloat16))


def solution(mesh):
    placed = (
        P("dp", None),
        P(None, "dp", "tensor"),
        P(None, "dp", None),
        P(None, "dp", "tensor"),
        P(None, "dp", "tensor"),
    )
    return jax.shard_map(
        on_device,
        mesh=mesh,
        in_specs=placed,
        out_specs=(P(None, "dp", "tensor"), P(None, "dp", "tensor"), P(None, "dp", "tensor")),
        check_vma=False,
    )
```

profile of v0, /device:TPU:2, one launch (start us, length us, event | category | flops | bytes accessed | tf_op | source)
XLA Modules:
  0.0 481.8 jit_solution(17600005652465332788)
XLA Ops:
  7.2 0.0 copy-start
  7.2 0.0 all-gather.3.cloned.1.call-start
  7.2 0.7 all-gather.3.cloned.1.call-update
  7.9 0.0 reduce-scatter.2.cloned.1.call-start
  8.0 140.9 %all-gather.3.cloned.1.call-done = bf16[3,5120,512]{2,1,0:T(8,128)(2,1)} async-done(((bf16[3,160,512]{2,1,0:T(8,128)(2,1)}), bf16[3,5120,512]{2,1,0:T(8,128)(2,1)}) %all-gather.3.cloned.1.call-update) | async-done | bytes 15728656 | tf_op jit(solution)/shard_map/all_gather | solution.py:18
  148.9 17.8 %fusion = f32[3,512,768]{2,1,0:T(8,128)S(1)} fusion(bf16[3,5120,512]{2,1,0:T(8,128)(2,1)} %all-gather.3.cloned.1.call-done, bf16[768,5120]{1,0:T(8,128)(2,1)} %param.5), kind=kOutput, calls=%fused_computation | convolution fusion | flops 12079595520 | bytes 28311552 | tf_op jit(solution)/shard_map/tr,krs->kts/dot_general | solution.py:15
  166.8 0.0 copy-done
  166.8 7.7 %fusion.5 = f32[3,512,640]{2,1,0:T(8,128)} fusion(f32[3,512,768]{2,1,0:T(8,128)S(1)} %fusion, bf16[3,768,640]{2,1,0:T(8,128)(2,1)S(1)} %copy-done), kind=kOutput, calls=%fused_computation.8 | convolution fusion | flops 9059696640 | bytes 11599872 | tf_op jit(solution)/shard_map/kts,ktc->ksc/dot_general | solution.py:21
  174.5 0.0 copy-start.1
  174.5 0.0 reduce-scatter.2.cloned.1.call-update
  174.5 0.0 all-gather.5.cloned.1.call-start
  174.5 217.9 %reduce-scatter.2.cloned.1.call-done = f32[3,16,640]{2,1,0:T(8,128)} async-done(((f32[3,512,640]{2,1,0:T(8,128)}), f32[3,16,640]{2,1,0:T(8,128)}) %reduce-scatter.2.cloned.1.call-update) | async-done | bytes 122896 | tf_op jit(solution)/shard_map/reduce_scatter | solution.py:24
  392.4 1.8 divide_convert_fusion
  394.2 0.0 all-gather.5.cloned.1.call-update
  394.2 78.1 %all-gather.5.cloned.1.call-done = bf16[3,512,640]{2,1,0:T(8,128)(2,1)} async-done(((bf16[3,16,640]{2,1,0:T(8,128)(2,1)}), bf16[3,512,640]{2,1,0:T(8,128)(2,1)}) %all-gather.5.cloned.1.call-update) | async-done | bytes 1966096 | tf_op jit(solution)/shard_map/all_gather | solution.py:34
  472.3 0.0 copy-done.1
  472.3 2.9 fusion.2
Async XLA Ops:
  7.2 159.6 %copy-start = (bf16[3,768,640]{2,1,0:T(8,128)(2,1)S(1)}, bf16[3,768,640]{2,1,0:T(8,128)(2,1)}, u32[]{:S(2)}) copy-start(bf16[3,768,640]{2,1,0:T(8,128)(2,1)} %param.6) | copy-start | bytes 8847364
  7.2 141.7 %all-gather.3.cloned.1.call-start = ((), (), s32[]{:S(2)}) async-start(), calls=%async_computation.1 | async-start | bytes 16220160 | tf_op jit(solution)/shard_map/all_gather | solution.py:18
  7.9 384.5 %reduce-scatter.2.cloned.1.call-start = ((), (), s32[]{:S(2)}) async-start(), calls=%async_computation.2 | async-start | bytes 4055040 | tf_op jit(solution)/shard_map/reduce_scatter | solution.py:24
  174.5 297.9 %copy-start.1 = (bf16[3,160,512]{2,1,0:T(8,128)(2,1)S(1)}, bf16[3,160,512]{2,1,0:T(8,128)(2,1)}, u32[]{:S(2)}) copy-start(bf16[3,160,512]{2,1,0:T(8,128)(2,1)} %param.7) | copy-start | bytes 1474564
  174.5 297.8 %all-gather.5.cloned.1.call-start = ((), (), s32[]{:S(2)}) async-start(), calls=%async_computation.3 | async-start | bytes 2027520 | tf_op jit(solution)/shard_map/all_gather | solution.py:34
Sparse Core Ops, SparseCore 0:
  10.6 138.2 all-gather.2
  174.6 217.8 reduce-scatter.1
  396.1 76.1 all-gather.4
where the time goes:
time: 482 us
  waiting for transfers between devices  438 us (91%)
  matrix products  28.5 us (6%)
  between operations  13.8 us (3%)
    reduce_scatter x1, waiting for transfers between devices, on_device(): lax.psum_scatter(grad_local, 'dp', scatter_dimension=1, tiled=True)  218 us
    all_gather x1, waiting for transfers between devices, on_device(): lax.all_gather(projector, 'dp', axis=1, tiled=True)  141 us
    all_gather x1, waiting for transfers between devices, on_device(): lax.all_gather(low_step, 'dp', axis=1, tiled=True)  78.1 us
    dot_general x1, matrix products, on_device(): jnp.einsum('tr,krs->kts', columns, lax.all_gather(projector, 'dp', axis=1...  17.8 us
  transfers between devices with their start and end apart: 3, of which 3 were waited for; matrix products, arithmetic and copies ran while one was open for 0% of the time, Pallas kernels for 0%

commit v1 on v0

--- a/solution.py
+++ b/solution.py
@@ -11,26 +11,24 @@
 
 
 def on_device(activations, cotangent, projector, first_moment, second_moment):
-    columns = activations
+    parts = lax.axis_size("tensor")
+    width = projector.shape[2] // parts
+    mine = lax.dynamic_slice_in_dim(projector, lax.axis_index("tensor") * width, width, axis=2)
+    gathered = lax.all_gather(mine, "dp", axis=1, tiled=True)
     lowered = jnp.einsum(
-        "tr,krs->kts",
-        columns,
-        lax.all_gather(projector, "dp", axis=1, tiled=True),
-        preferred_element_type=jnp.float32,
-    )
-    grad_local = jnp.einsum(
-        "kts,ktc->ksc", lowered, cotangent.astype(jnp.float32), precision=lax.Precision.HIGHEST
-    )
+        "tr,krs->kts", activations, gathered, preferred_element_type=jnp.float32
+    ).astype(jnp.bfloat16)
+    lowered = lax.all_gather(lowered, "tensor", axis=2, tiled=True)
+    grad_local = jnp.einsum("kts,ktc->ksc", lowered, cotangent, preferred_element_type=jnp.float32)
     grad_owned = lax.psum_scatter(grad_local, "dp", scatter_dimension=1, tiled=True)
     fresh_first = beta_one * first_moment + (1.0 - beta_one) * grad_owned
     fresh_second = beta_two * second_moment + (1.0 - beta_two) * grad_owned * grad_owned
     low_step = (fresh_first / bias_one / (jnp.sqrt(fresh_second / bias_two) + adam_eps)).astype(
         jnp.bfloat16
     )
-    columns = projector
     expanded = jnp.einsum(
         "krs,ksc->krc",
-        columns,
+        projector,
         lax.all_gather(low_step, "dp", axis=1, tiled=True),
         preferred_element_type=jnp.float32,
     )

time: 482 us -> 446 us (0.925)
  waiting for transfers between devices: 438 us -> 411 us
  matrix products: 28.5 us -> 17.1 us
    all_gather x1 -> x2, waiting for transfers between devices: 141 us -> 111 us  [the longest x1 86.2 us: on_device(): gathered = lax.all_gather(mine, 'dp', axis=1, tiled=True)]
    dot_general x3, matrix products: 28.5 us -> 17.1 us  [the longest x1 8.6 us: on_device(): jnp.einsum('tr,krs->kts', activations, gathered, preferred_element_type=j...]
    reduce_scatter x1, waiting for transfers between devices: 218 us -> 223 us  [on_device(): lax.psum_scatter(grad_local, 'dp', scatter_dimension=1, tiled=True)]
  transfers between devices with their start and end apart: 3 -> 4, of which waited for: 3 -> 4; matrix products, arithmetic and copies ran while one was open for 0% -> 0% of each run, Pallas kernels for 0% -> 0%
where the time goes in v1:
time: 446 us
  waiting for transfers between devices  411 us (92%)
  matrix products  17.1 us (4%)
  between operations  13.8 us (3%)
    reduce_scatter x1, waiting for transfers between devices, on_device(): lax.psum_scatter(grad_local, 'dp', scatter_dimension=1, tiled=True)  223 us
    all_gather x1, waiting for transfers between devices, on_device(): gathered = lax.all_gather(mine, 'dp', axis=1, tiled=True)  86.2 us
    all_gather x1, waiting for transfers between devices, on_device(): lax.all_gather(low_step, 'dp', axis=1, tiled=True)  77.9 us
    all_gather x1, waiting for transfers between devices, on_device(): lowered = lax.all_gather(lowered, 'tensor', axis=2, tiled=True)  24.4 us
  transfers between devices with their start and end apart: 4, of which 4 were waited for; matrix products, arithmetic and copies ran while one was open for 0% of the time, Pallas kernels for 0%

profile of v1, /device:TPU:2, one launch (start us, length us, event | category | flops | bytes accessed | tf_op | source)
XLA Modules:
  0.0 445.9 jit_solution(1320347820525907544)
XLA Ops:
  7.2 0.0 copy-start
  7.2 0.0 all-gather.4.cloned.1.call-start
  7.2 1.8 constant_dynamic-slice_fusion
  9.0 0.0 all-gather.4.cloned.1.call-update
  9.1 0.0 all-gather.6.cloned.1.call-start
  9.1 86.2 %all-gather.4.cloned.1.call-done = bf16[3,5120,64]{2,1,0:T(8,128)(2,1)} async-done(((bf16[3,160,64]{2,1,0:T(8,128)(2,1)}), bf16[3,5120,64]{2,1,0:T(8,128)(2,1)}) %all-gather.4.cloned.1.call-update) | async-done | bytes 1966096 | tf_op jit(solution)/shard_map/all_gather | solution.py:17
  95.3 8.6 %fusion.6 = bf16[3,768,64]{1,2,0:T(8,128)(2,1)} fusion(bf16[3,5120,64]{2,1,0:T(8,128)(2,1)} %all-gather.4.cloned.1.call-done, bf16[768,5120]{1,0:T(8,128)(2,1)} %param.5), kind=kOutput, calls=%fused_computation.5 | convolution fusion | flops 1510096896 | bytes 10125312 | tf_op jit(solution)/shard_map/tr,krs->kts/dot_general | solution.py:18
  103.9 0.0 all-gather.6.cloned.1.call-update
  103.9 0.0 reduce-scatter.2.cloned.1.call-start
  104.0 24.4 %all-gather.6.cloned.1.call-done = bf16[3,768,512]{1,2,0:T(8,128)(2,1)} async-done(((bf16[3,768,64]{1,2,0:T(8,128)(2,1)}), bf16[3,768,512]{1,2,0:T(8,128)(2,1)}) %all-gather.6.cloned.1.call-update) | async-done | bytes 2359312 | tf_op jit(solution)/shard_map/all_gather | solution.py:21
  128.3 0.0 copy-done
  128.3 5.5 %fusion.11 = f32[3,512,640]{2,1,0:T(8,128)} fusion(bf16[3,768,512]{1,2,0:T(8,128)(2,1)} %all-gather.6.cloned.1.call-done, bf16[3,768,640]{2,1,0:T(8,128)(2,1)S(1)} %copy-done), kind=kOutput, calls=%fused_computation.11 | convolution fusion | flops 1509949440 | bytes 9240576 | tf_op jit(solution)/shard_map/kts,ktc->ksc/dot_general | solution.py:22
  133.8 0.0 copy-start.1
  133.8 0.0 reduce-scatter.2.cloned.1.call-update
  133.9 0.0 all-gather.8.cloned.1.call-start
  133.9 222.8 %reduce-scatter.2.cloned.1.call-done = f32[3,16,640]{2,1,0:T(8,128)} async-done(((f32[3,512,640]{2,1,0:T(8,128)}), f32[3,16,640]{2,1,0:T(8,128)}) %reduce-scatter.2.cloned.1.call-update) | async-done | bytes 122896 | tf_op jit(solution)/shard_map/reduce_scatter | solution.py:23
  356.7 1.8 divide_convert_fusion
  358.5 0.0 all-gather.8.cloned.1.call-update
  358.5 77.9 %all-gather.8.cloned.1.call-done = bf16[3,512,640]{2,1,0:T(8,128)(2,1)} async-done(((bf16[3,16,640]{2,1,0:T(8,128)(2,1)}), bf16[3,512,640]{2,1,0:T(8,128)(2,1)}) %all-gather.8.cloned.1.call-update) | async-done | bytes 1966096 | tf_op jit(solution)/shard_map/all_gather | solution.py:32
  436.4 0.0 copy-done.1
  436.4 2.9 fusion.2
Async XLA Ops:
  7.2 121.2 %copy-start = (bf16[3,768,640]{2,1,0:T(8,128)(2,1)S(1)}, bf16[3,768,640]{2,1,0:T(8,128)(2,1)}, u32[]{:S(2)}) copy-start(bf16[3,768,640]{2,1,0:T(8,128)(2,1)} %param.6) | copy-start | bytes 8847364
  7.2 88.1 %all-gather.4.cloned.1.call-start = ((), (), s32[]{:S(2)}) async-start(), calls=%async_computation.1 | async-start | bytes 4055040 | tf_op jit(solution)/shard_map/all_gather | solution.py:17
  9.1 119.2 %all-gather.6.cloned.1.call-start = ((), (), s32[]{:S(2)}) async-start(), calls=%async_computation.2 | async-start | bytes 2654208 | tf_op jit(solution)/shard_map/all_gather | solution.py:21
  103.9 252.8 %reduce-scatter.2.cloned.1.call-start = ((), (), s32[]{:S(2)}) async-start(), calls=%async_computation.3 | async-start | bytes 4055040 | tf_op jit(solution)/shard_map/reduce_scatter | solution.py:23
  133.8 302.6 %copy-start.1 = (bf16[3,160,512]{2,1,0:T(8,128)(2,1)S(1)}, bf16[3,160,512]{2,1,0:T(8,128)(2,1)}, u32[]{:S(2)}) copy-start(bf16[3,160,512]{2,1,0:T(8,128)(2,1)} %param.7) | copy-start | bytes 1474564
  133.9 302.5 %all-gather.8.cloned.1.call-start = ((), (), s32[]{:S(2)}) async-start(), calls=%async_computation.4 | async-start | bytes 2027520 | tf_op jit(solution)/shard_map/all_gather | solution.py:32
Sparse Core Ops, SparseCore 0:
  11.2 84.0 all-gather.3
  104.0 24.2 all-gather.5
  134.0 222.6 reduce-scatter.1
  360.2 76.1 all-gather.7

commit v2 on v1

v2 whole, which is shorter than its diff:
```python
import jax
import jax.numpy as jnp
from jax import lax
from jax.experimental import pallas as pl
from jax.experimental.pallas import tpu as pltpu
from jax.sharding import PartitionSpec as P

beta_one = 0.9
beta_two = 0.95
adam_eps = 1e-08
bias_one = 1.0 - 0.9**10
bias_two = 1.0 - 0.95**10

MESH = pl.DeviceIdType.MESH
f32, bf16 = jnp.float32, jnp.bfloat16
NK, NY, NZ, NX = 3, 4, 8, 4
TOK, HALF = 768, 384
ROWS, SHARE = 160, 80
BIG, SMALL = 64, 16
SLAB = NZ * ROWS
LANES = 128
COLS, WIDE = 640, 512
OWN = 16

Z_P0, Z_P1, Z_R0, Z_R1, Z_L0, Z_L1 = range(6)
Y_P0, Y_P1, Y_R0, Y_R1, Y_L0, Y_L1 = range(6)


def kernel(
    p_ref, m1_ref, m2_ref, a_hbm, g_hbm,
    nf_ref, ns_ref, u_ref,
    pg, av, gv, acc, lt, gr, rb0, rb1, s0, s1, q0, q1, lg,
    zs, zr, ys, yr, cs, cr, xs, xr, ds, dr, lsem,
):
    dp, tensor = lax.axis_index("dp"), lax.axis_index("tensor")
    y, z, x, c = dp // NZ, dp % NZ, tensor // 2, tensor % 2

    load_a = pltpu.make_async_copy(
        a_hbm.at[pl.ds(pl.multiple_of(c * HALF, HALF), HALF)], av, lsem.at[0]
    )
    load_g = pltpu.make_async_copy(g_hbm, gv, lsem.at[1])

    def at_z(d):
        return (y * NZ + (z + d) % NZ, tensor)

    def at_y(d):
        return (((y + d) % NY) * NZ + z, tensor)

    def at_x(d):
        return (dp, ((x + d) % NX) * 2 + c)

    partner = (dp, x * 2 + (1 - c))

    barrier = pltpu.get_barrier_semaphore()

    def greet(who):
        pl.semaphore_signal(barrier, inc=1, device_id=who, device_id_type=MESH)

    for d in range(1, NZ):
        greet(at_z(d))
    for d in range(1, NY):
        greet(at_y(d))
    for d in range(1, NX):
        greet(at_x(d))
    greet(partner)
    load_a.start()
    load_g.start()

    rows0 = pl.ds(pl.multiple_of(c * SHARE, 16), BIG)
    rows1 = pl.ds(pl.multiple_of(c * SHARE + BIG, 16), SMALL)
    share = pl.ds(pl.multiple_of(c * SHARE, 16), SHARE)
    mine = pl.ds(pl.multiple_of(x * LANES, LANES), LANES)
    toks = pl.ds(pl.multiple_of(c * HALF, HALF), HALF)
    low, high = pl.ds(0, WIDE), pl.ds(WIDE, COLS - WIDE)

    def copy(src, dst, send, recv, who):
        return pltpu.make_async_remote_copy(
            src_ref=src, dst_ref=dst, send_sem=send, recv_sem=recv,
            device_id=who, device_id_type=MESH,
        )

    def z_refs(kind, k, d):
        to = (z + d) % NZ
        if kind == Z_P0:
            return p_ref.at[k, rows0, mine], pg.at[k, y, z, rows0]
        if kind == Z_P1:
            here = pg.at[k, :, z, rows1]
            return here, here
        if kind == Z_R0:
            return s0.at[k, to], q0.at[k, d]
        if kind == Z_R1:
            return gr.at[k, :, to, :, high], rb1.at[k, d]
        if kind == Z_L0:
            here = lg.at[k, y, z, :, low]
            return here, here
        here = lg.at[k, :, z, :, high]
        return here, here

    def y_refs(kind, k, d):
        to = (y + d) % NY
        if kind == Y_P0:
            here = pg.at[k, y, :, rows0]
            return here, here
        if kind == Y_P1:
            return p_ref.at[k, rows1, mine], pg.at[k, y, z, rows1]
        if kind == Y_R0:
            return gr.at[k, to, :, :, low], rb0.at[k, d]
        if kind == Y_R1:
            return s1.at[k, to], q1.at[k, d]
        if kind == Y_L0:
            here = lg.at[k, y, :, :, low]
            return here, here
        here = lg.at[k, y, z, :, high]
        return here, here

    def z_copy(kind, k, d):
        src, dst = z_refs(kind, k, d)
        return copy(src, dst, zs.at[kind, k, d], zr.at[kind, k, d], at_z(d))

    def y_copy(kind, k, d):
        src, dst = y_refs(kind, k, d)
        return copy(src, dst, ys.at[kind, k, d], yr.at[kind, k, d], at_y(d))

    def c_copy(k, i):
        if isinstance(i, int) and i == NY:
            here = pg.at[k, :, :, rows1]
        else:
            here = pg.at[k, (y + NY - i) % NY, :, rows0]
        return copy(here, here, cs.at[k, i], cr.at[k, i], partner)

    def x_copy(k, d):
        here = lt.at[k, x, :, toks]
        return copy(here, here, xs.at[k, d], xr.at[k, d], at_x(d))

    def d_copy(k, d):
        here = lt.at[k, (x + NX - d) % NX, :, toks]
        return copy(here, here, ds.at[k, d], dr.at[k, d], partner)

    def each(n, act):
        def body(d, carry):
            act(d)
            return carry

        lax.fori_loop(1, n, body, 0)

    def z_start(kind, k):
        each(NZ, lambda d: z_copy(kind, k, d).start())

    def z_arrive(kind, k):
        each(NZ, lambda d: z_copy(kind, k, d).wait_recv())

    def y_start(kind, k):
        each(NY, lambda d: y_copy(kind, k, d).start())

    def y_arrive(kind, k):
        each(NY, lambda d: y_copy(kind, k, d).wait_recv())

    def gather_first(k):
        z_start(Z_P0, k)
        y_start(Y_P1, k)
        pg[k, y, z, share] = p_ref[k, share, mine]

    def gather_second(k):
        y_arrive(Y_P1, k)
        z_start(Z_P1, k)
        z_arrive(Z_P0, k)
        y_start(Y_P0, k)
        c_copy(k, 0).start()

    def add_slab(k, d, first=False):
        at = (y + NY - d) % NY
        part = jnp.dot(
            av[:, pl.ds(pl.multiple_of(at * SLAB, LANES), SLAB)],
            pg[k, at].reshape(SLAB, LANES),
            preferred_element_type=f32,
        )
        acc[...] = part if first else acc[...] + part

    def lower(k):
        z_arrive(Z_P1, k)
        c_copy(k, NY).start()
        if k == 0:
            load_a.wait()
        c_copy(k, NY).wait_recv()
        c_copy(k, 0).wait_recv()
        add_slab(k, 0, True)
        y_copy(Y_P0, k, 1).wait_recv()
        c_copy(k, 1).start()
        y_copy(Y_P0, k, 3).wait_recv()
        c_copy(k, 3).start()
        c_copy(k, 1).wait_recv()
        add_slab(k, 1)
        y_copy(Y_P0, k, 2).wait_recv()
        c_copy(k, 2).start()
        c_copy(k, 3).wait_recv()
        add_slab(k, 3)
        c_copy(k, 2).wait_recv()
        add_slab(k, 2)
        lt[k, x, :, toks] = acc[...].T.astype(bf16)
        each(NX, lambda d: x_copy(k, d).start())
        d_copy(k, 0).start()

    def grad_slab(k, d):
        at = (x + NX - d) % NX
        part = jnp.dot(lt[k, at], gv[k], preferred_element_type=f32)
        gr[k, at] = part.astype(bf16).reshape(NZ, OWN, COLS)

        @pl.when(at != y)
        def _():
            y_copy(Y_R0, k, (at + NY - y) % NY).start()

    def grad(k):
        if k == 0:
            load_g.wait()
        d_copy(k, 0).wait_recv()
        grad_slab(k, 0)
        x_copy(k, 1).wait_recv()
        d_copy(k, 1).start()
        x_copy(k, 3).wait_recv()
        d_copy(k, 3).start()
        d_copy(k, 1).wait_recv()
        grad_slab(k, 1)
        x_copy(k, 2).wait_recv()
        d_copy(k, 2).start()
        d_copy(k, 3).wait_recv()
        grad_slab(k, 3)
        d_copy(k, 2).wait_recv()
        grad_slab(k, 2)
        z_start(Z_R1, k)

    def reduce_second(k):
        z_arrive(Z_R1, k)
        total = gr[k, :, z, :, high].astype(f32)
        for d in range(1, NZ):
            total += rb1[k, d].astype(f32)
        s1[k] = total.astype(bf16)
        y_start(Y_R1, k)
        y_arrive(Y_R0, k)
        total = gr[k, y, :, :, low].astype(f32)
        for d in range(1, NY):
            total += rb0[k, d].astype(f32)
        s0[k] = total.astype(bf16)
        z_start(Z_R0, k)

    def step(k, cols, grad_owned):
        first = beta_one * m1_ref[k, :, cols] + (1.0 - beta_one) * grad_owned
        second = beta_two * m2_ref[k, :, cols] + (1.0 - beta_two) * grad_owned * grad_owned
        nf_ref[k, :, cols] = first
        ns_ref[k, :, cols] = second
        low_step = first / bias_one / (jnp.sqrt(second / bias_two) + adam_eps)
        lg[k, y, z, :, cols] = low_step.astype(bf16)

    def moments(k):
        y_arrive(Y_R1, k)
        total = s1[k, y].astype(f32)
        for d in range(1, NY):
            total += q1[k, d].astype(f32)
        step(k, high, total)
        y_start(Y_L1, k)
        z_arrive(Z_R0, k)
        total = s0[k, z].astype(f32)
        for d in range(1, NZ):
            total += q0[k, d].astype(f32)
        step(k, low, total)
        z_start(Z_L0, k)

    def spread_second(k):
        y_arrive(Y_L1, k)
        z_start(Z_L1, k)
        z_arrive(Z_L0, k)
        y_start(Y_L0, k)

    def update(k):
        z_arrive(Z_L1, k)
        y_arrive(Y_L0, k)
        whole = lg[k].reshape(NY * NZ * OWN, COLS)
        u_ref[k] = jnp.dot(p_ref[k], whole, preferred_element_type=f32).astype(bf16)

    pl.semaphore_wait(barrier, NZ - 1 + NY - 1 + NX - 1 + 1)

    for what, k in (
        (gather_first, 0), (gather_first, 1), (gather_first, 2),
        (gather_second, 0), (gather_second, 1), (gather_second, 2),
        (lower, 0), (lower, 1), (grad, 0), (lower, 2), (grad, 1), (reduce_second, 0),
        (grad, 2), (moments, 0), (reduce_second, 1), (spread_second, 0),
        (moments, 1), (reduce_second, 2), (update, 0), (spread_second, 1),
        (moments, 2), (update, 1), (spread_second, 2), (update, 2),
    ):
        what(k)

    for k in range(NK):
        for kind in range(6):
            each(NZ, lambda d: z_copy(kind, k, d).wait_send())
            each(NY, lambda d: y_copy(kind, k, d).wait_send())
        for i in range(NY + 1):
            c_copy(k, i).wait_send()
        for d in range(NX):
            d_copy(k, d).wait_send()
        each(NX, lambda d: x_copy(k, d).wait_send())


def on_device(activations, cotangent, projector, first_moment, second_moment):
    vmem = pl.BlockSpec(memory_space=pltpu.VMEM)
    hbm = pl.BlockSpec(memory_space=pl.ANY)
    dma = pltpu.SemaphoreType.DMA
    return pl.pallas_call(
        kernel,
        out_shape=(
            jax.ShapeDtypeStruct((NK, OWN, COLS), f32),
            jax.ShapeDtypeStruct((NK, OWN, COLS), f32),
            jax.ShapeDtypeStruct((NK, ROWS, COLS), bf16),
        ),
        in_specs=[vmem, vmem, vmem, hbm, hbm],
        out_specs=(vmem, vmem, vmem),
        scratch_shapes=[
            pltpu.VMEM((NK, NY, NZ, ROWS, LANES), bf16),
            pltpu.VMEM((HALF, NY * SLAB), bf16),
            pltpu.VMEM((NK, TOK, COLS), bf16),
            pltpu.VMEM((HALF, LANES), f32),
            pltpu.VMEM((NK, NX, LANES, TOK), bf16),
            pltpu.VMEM((NK, NY, NZ, OWN, COLS), bf16),
            pltpu.VMEM((NK, NY, NZ, OWN, WIDE), bf16),
            pltpu.VMEM((NK, NZ, NY, OWN, COLS - WIDE), bf16),
            pltpu.VMEM((NK, NZ, OWN, WIDE), bf16),
            pltpu.VMEM((NK, NY, OWN, COLS - WIDE), bf16),
            pltpu.VMEM((NK, NZ, OWN, WIDE), bf16),
            pltpu.VMEM((NK, NY, OWN, COLS - WIDE), bf16),
            pltpu.VMEM((NK, NY, NZ, OWN, COLS), bf16),
            dma((6, NK, NZ)), dma((6, NK, NZ)),
            dma((6, NK, NY)), dma((6, NK, NY)),
            dma((NK, NY + 1)), dma((NK, NY + 1)),
            dma((NK, NX)), dma((NK, NX)),
            dma((NK, NX)), dma((NK, NX)),
            dma((2,)),
        ],
        compiler_params=pltpu.CompilerParams(
            collective_id=0, has_side_effects=True, vmem_limit_bytes=44 * 2**20
        ),
        name="galore_step",
    )(projector, first_moment, second_moment, activations, cotangent)


def solution(mesh):
    placed = (
        P("dp", None),
        P(None, "dp", "tensor"),
        P(None, "dp", None),
        P(None, "dp", "tensor"),
        P(None, "dp", "tensor"),
    )
    return jax.shard_map(
        on_device,
        mesh=mesh,
        in_specs=placed,
        out_specs=(P(None, "dp", "tensor"), P(None, "dp", "tensor"), P(None, "dp", "tensor")),
        check_vma=False,
    )
```

time: 446 us -> 102 us (0.23)
  waiting for transfers between devices: 411 us -> 0 us
  Pallas kernels: 0 us -> 93.6 us
  matrix products: 17.1 us -> 0 us
  between operations: 13.8 us -> 0.65 us
  local copies, waits for them, and re-layouts: 1.82 us -> 6.78 us
    reduce_scatter x1 -> x0, waiting for transfers between devices: 223 us -> none  [on_device(): lax.psum_scatter(grad_local, 'dp', scatter_dimension=1, tiled=True)]
    all_gather x3 -> x0, waiting for transfers between devices: 188 us -> none  [the longest x1 86.2 us: on_device(): gathered = lax.all_gather(mine, 'dp', axis=1, tiled=True)]
    pallas_call x0 -> x1, Pallas kernels: none -> 93.6 us  [on_device(): pl.pallas_call(kernel, out_shape=(jax.ShapeDtypeStruct((NK, OWN, COLS), f...]
    dot_general x3 -> x0, matrix products: 17.1 us -> none  [the longest x1 8.6 us: on_device(): jnp.einsum('tr,krs->kts', activations, gathered, preferred_element_type=j...]
    unnamed x4 -> x11, local copies, waits for them, and re-layouts: 0.01 us -> 6.78 us
  transfers between devices with their start and end apart: 4 -> 0, of which waited for: 4 -> 0; matrix products, arithmetic and copies ran while one was open for 0% -> 0% of each run, Pallas kernels for 0% -> 0%
where the time goes in v2:
time: 102 us; the launch traced here: 101 us
  Pallas kernels  93.6 us (92%)
  local copies, waits for them, and re-layouts  6.78 us (7%)
    pallas_call x1, Pallas kernels, on_device(): pl.pallas_call(kernel, out_shape=(jax.ShapeDtypeStruct((NK, OWN, COLS), f...  93.6 us
    unnamed x11, local copies, waits for them, and re-layouts  6.78 us

profile of v2, /device:TPU:2, one launch (start us, length us, event | category | flops | bytes accessed | tf_op | source)
XLA Modules:
  0.0 101.0 jit_solution(8919432813808321907)
XLA Ops:
  0.6 0.0 copy-start
  0.6 1.8 %copy-done = bf16[3,768,640]{2,1,0:T(8,128)(2,1)S(1)} copy-done((bf16[3,768,640]{2,1,0:T(8,128)(2,1)S(1)}, bf16[3,768,640]{2,1,0:T(8,128)(2,1)}, u32[]{:S(2)}) %copy-start) | copy-done | bytes 2949144
  2.5 0.0 copy-start.1
  2.5 1.0 %copy-done.1 = bf16[3,160,512]{2,1,0:T(8,128)(2,1)S(1)} copy-done((bf16[3,160,512]{2,1,0:T(8,128)(2,1)S(1)}, bf16[3,160,512]{2,1,0:T(8,128)(2,1)}, u32[]{:S(2)}) %copy-start.1) | copy-done | bytes 491544
  3.5 0.0 copy-start.2
  3.5 0.9 copy-done.2
  4.4 0.0 copy-start.3
  4.4 0.9 copy-done.3
  5.3 93.6 %galore_step.1 = (f32[3,16,640]{2,1,0:T(8,128)S(1)}, f32[3,16,640]{2,1,0:T(8,128)S(1)}, bf16[3,160,640]{2,1,0:T(8,128)(2,1)S(1)}) custom-call(bf16[3,160,512]{2,1,0:T(8,128)(2,1)S(1)} %copy-done.1, f32[3,16,640]{2,1,0:T(8,128)S(1)} %copy-done.2, f32[3,16,640]{2,1,0:T(8,128)S(1)} %copy-done.3, bf16[768,5120]{1,0:T(8,128)(2,1)} %a_hbm.1, ...), custom_call_target="tpu_custom_call" | custom-call | tf_op jit(solution)/shard_map/galore_step/pallas_call | solution.py:306
  98.9 0.7 copy.11
  99.6 0.6 copy.12
  100.2 0.8 copy.13
Async XLA Ops:
  0.6 1.8 %copy-start = (bf16[3,768,640]{2,1,0:T(8,128)(2,1)S(1)}, bf16[3,768,640]{2,1,0:T(8,128)(2,1)}, u32[]{:S(2)}) copy-start(bf16[3,768,640]{2,1,0:T(8,128)(2,1)} %g_hbm.1) | copy-start | bytes 8847364
  2.5 1.0 %copy-start.1 = (bf16[3,160,512]{2,1,0:T(8,128)(2,1)S(1)}, bf16[3,160,512]{2,1,0:T(8,128)(2,1)}, u32[]{:S(2)}) copy-start(bf16[3,160,512]{2,1,0:T(8,128)(2,1)} %p_ref.1) | copy-start | bytes 1474564
  3.5 0.9 copy-start.2
  4.4 0.9 copy-start.3

commit v3 on v2

v3 whole, which is shorter than its diff:
```python
import jax
import jax.numpy as jnp
from jax import lax
from jax.experimental import pallas as pl
from jax.experimental.pallas import tpu as pltpu
from jax.sharding import PartitionSpec as P

beta_one = 0.9
beta_two = 0.95
adam_eps = 1e-08
bias_one = 1.0 - 0.9**10
bias_two = 1.0 - 0.95**10

MESH = pl.DeviceIdType.MESH
f32, bf16 = jnp.float32, jnp.bfloat16
NK, NY, NZ, NX = 3, 4, 8, 4
TOK, HALF = 768, 384
ROWS, SHARE = 160, 80
BIG, SMALL = 64, 16
SLAB = NZ * ROWS
LANES = 128
COLS, WIDE = 640, 512
OWN = 16

Z_ORDER = (1, 7, 2, 6, 3, 5, 4)
Z_COME = (1, 7, 2, 6, 3, 5, 4)
Z_P0, Z_P1, Z_R0, Z_R1, Z_L0, Z_L1 = range(6)
Y_P0, Y_P1, Y_R0, Y_R1, Y_L0, Y_L1, Y_R2, Y_U = range(8)


def kernel(
    p_hbm, m1_hbm, m2_hbm, a_hbm, g_hbm,
    nf_ref, ns_ref, u_ref,
    p_ref, m1_ref, m2_ref, pg, av, gv, acc, lt, gr, rb0, rb1, s0, s1, q0, q1, lown, la, lb, p4, uq,
    zs, zr, zpr, ys, yr, ypr, cs, cr, xs, xr, ds, dr, ps, pr, es, er, lsem,
):
    dp, tensor = lax.axis_index("dp"), lax.axis_index("tensor")
    y, z, x, c = dp // NZ, dp % NZ, tensor // 2, tensor % 2

    load_a = pltpu.make_async_copy(
        a_hbm.at[pl.ds(pl.multiple_of(c * HALF, HALF), HALF)], av, lsem.at[0]
    )
    load_g = pltpu.make_async_copy(g_hbm, gv, lsem.at[1])
    load_p = pltpu.make_async_copy(p_hbm, p_ref, lsem.at[2])
    load_m1 = pltpu.make_async_copy(m1_hbm, m1_ref, lsem.at[3])
    load_m2 = pltpu.make_async_copy(m2_hbm, m2_ref, lsem.at[4])
    load_p.start()

    zt = [lax.rem(z + d, NZ) for d in range(NZ)]
    yt = [lax.rem(y + d, NY) for d in range(NY)]
    xt = [lax.rem(x + d, NX) for d in range(NX)]
    at_z = [(y * NZ + zt[d], tensor) for d in range(NZ)]
    at_y = [(yt[d] * NZ + z, tensor) for d in range(NY)]
    at_x = [(dp, xt[d] * 2 + c) for d in range(NX)]
    partner = (dp, x * 2 + (1 - c))

    barrier = pltpu.get_barrier_semaphore()

    def greet(who):
        pl.semaphore_signal(barrier, inc=1, device_id=who, device_id_type=MESH)

    for d in range(1, NZ):
        greet(at_z[d])
    for d in range(1, NY):
        greet(at_y[d])
    for d in range(1, NX):
        greet(at_x[d])
    greet(partner)
    load_a.start()
    load_g.start()
    load_m1.start()
    load_m2.start()

    rows0 = pl.ds(pl.multiple_of(c * SHARE, 16), BIG)
    rows1 = pl.ds(pl.multiple_of(c * SHARE + BIG, 16), SMALL)
    share = pl.ds(pl.multiple_of(c * SHARE, 16), SHARE)
    mine = pl.ds(pl.multiple_of(x * LANES, LANES), LANES)
    toks = pl.ds(pl.multiple_of(c * HALF, HALF), HALF)
    low, high = pl.ds(0, WIDE), pl.ds(WIDE, COLS - WIDE)

    def copy(src, dst, send, recv, who):
        return pltpu.make_async_remote_copy(
            src_ref=src, dst_ref=dst, send_sem=send, recv_sem=recv,
            device_id=who, device_id_type=MESH,
        )

    def z_copy(kind, k, d):
        to = zt[d]
        if kind == Z_P0:
            src, dst = p_ref.at[k, rows0, mine], pg.at[k, y, z, rows0]
        elif kind == Z_P1:
            src = dst = pg.at[k, :, z, rows1]
        elif kind == Z_R1:
            src, dst = gr.at[k, :, to, :, high], rb1.at[k, d]
        elif kind == Z_L0:
            src = dst = la.at[k, :, z]
        else:
            src = dst = lb.at[k, y, z]
        recv = zpr.at[k, d] if kind == Z_P0 else zr.at[kind, k]
        return copy(src, dst, zs.at[kind, k], recv, at_z[d])

    def y_copy(kind, k, d):
        to = yt[d]
        if kind == Y_P1:
            src, dst = p_ref.at[k, rows1, mine], pg.at[k, y, z, rows1]
        elif kind == Y_R1:
            src, dst = s1.at[k, to], q1.at[k, d]
        elif kind == Y_L0:
            src, dst = lown.at[k, to], la.at[k, y, z]
        elif kind == Y_L1:
            src = dst = lb.at[k, y]
        else:
            quarter = pl.ds(pl.multiple_of(y * LANES, LANES), LANES)
            src, dst = uq.at[k, to], u_ref.at[k, :, quarter]
        return copy(src, dst, ys.at[kind, k], yr.at[kind, k], at_y[d])

    def y_block(k, at):
        here = pg.at[k, y, at, rows0]
        for d in (2, 1, 3):
            copy(here, here, ys.at[Y_P0, k], ypr.at[k, d], at_y[d]).start()

    def y_slab(k, d):
        here = pg.at[k, yt[(NY - d) % NY], :, rows0]
        return copy(here, here, ys.at[Y_P0, k], ypr.at[k, d], partner)

    def c_copy(k, i):
        here = pg.at[k, :, :, rows1] if i == NY else pg.at[k, yt[(NY - i) % NY], :, rows0]
        return copy(here, here, cs.at[k], cr.at[k, i], partner)

    def x_copy(k, d):
        here = lt.at[k, x, :, toks]
        return copy(here, here, xs.at[k], xr.at[k, d], at_x[d])

    def d_copy(k, d):
        here = lt.at[k, xt[(NX - d) % NX], :, toks]
        return copy(here, here, ds.at[k], dr.at[k, d], partner)

    def p_copy(k, d):
        return copy(pg.at[k, :, z, share], p4.at[k, :, share, mine], ps.at[k], pr.at[k], at_x[d])

    def e_copy(k):
        here = p4.at[k, :, share]
        return copy(here, here, es.at[k], er.at[k], partner)

    def z_all(kind, k):
        some = pl.ds(1, NZ - 1)
        whole = {
            Z_P0: pg.at[k, 0, some, pl.ds(0, BIG)],
            Z_P1: pg.at[k, :, some, rows1],
            Z_R0: q0.at[k, some],
            Z_R1: rb1.at[k, some],
            Z_L0: la.at[k, :, some],
            Z_L1: lb.at[k, y, some],
        }[kind]
        return copy(whole, whole, zs.at[kind, k], zr.at[kind, k], partner)

    def y_all(kind, k):
        some = pl.ds(1, NY - 1)
        whole = {
            Y_P0: pg.at[k, some, :, pl.ds(0, BIG)],
            Y_P1: pg.at[k, some, z, rows1],
            Y_R0: rb0.at[k, some, pl.ds(0, NZ // 2)],
            Y_R2: rb0.at[k, some, pl.ds(NZ // 2, NZ // 2)],
            Y_R1: q1.at[k, some],
            Y_L0: la.at[k, some, z],
            Y_L1: lb.at[k, some],
            Y_U: uq.at[k, some],
        }[kind]
        return copy(whole, whole, ys.at[kind, k], yr.at[kind, k], partner)

    def x_all(k):
        whole = lt.at[k, pl.ds(1, NX - 1), :, pl.ds(0, HALF)]
        return copy(whole, whole, xs.at[k], xr.at[k, 0], partner)

    def p_all(k):
        whole = pg.at[k, :, pl.ds(1, NX - 1), pl.ds(0, SHARE)]
        return copy(whole, whole, ps.at[k], pr.at[k], partner)

    def c_all(k):
        whole = pg.at[k, :, :, pl.ds(0, SHARE)]
        return copy(whole, whole, cs.at[k], cr.at[k, 0], partner)

    def d_all(k):
        whole = lt.at[k, :, :, pl.ds(0, HALF)]
        return copy(whole, whole, ds.at[k], dr.at[k, 0], partner)

    def z_start(kind, k):
        for d in Z_ORDER:
            z_copy(kind, k, d).start()

    def z_arrive(kind, k):
        z_all(kind, k).wait_recv()

    def y_start(kind, k):
        for d in (2, 1, 3):
            y_copy(kind, k, d).start()

    def y_arrive(kind, k):
        y_all(kind, k).wait_recv()

    def gather_first(k):
        if k:
            z_all(Z_P0, k - 1).wait_send()
        z_start(Z_P0, k)
        y_start(Y_P1, k)
        pg[k, y, z, share] = p_ref[k, share, mine]
        y_block(k, z)

    def gather_second(k):
        y_arrive(Y_P1, k)
        z_start(Z_P1, k)
        for d in Z_COME:
            z_copy(Z_P0, k, d).wait_recv()
            y_block(k, zt[NZ - d])
        c_copy(k, 0).start()

    def add_slab(k, d, first=False):
        at = yt[(NY - d) % NY]
        part = jnp.dot(
            av[:, pl.ds(pl.multiple_of(at * SLAB, LANES), SLAB)],
            pg[k, at].reshape(SLAB, LANES),
            preferred_element_type=f32,
        )
        acc[...] = part if first else acc[...] + part

    def lower(k):
        z_arrive(Z_P1, k)
        c_copy(k, NY).start()
        if k == 0:
            load_a.wait()
        c_copy(k, NY).wait_recv()
        c_copy(k, 0).wait_recv()
        add_slab(k, 0, True)
        y_slab(k, 1).wait_recv()
        c_copy(k, 1).start()
        y_slab(k, 3).wait_recv()
        c_copy(k, 3).start()
        c_copy(k, 1).wait_recv()
        add_slab(k, 1)
        y_slab(k, 2).wait_recv()
        c_copy(k, 2).start()
        c_copy(k, 3).wait_recv()
        add_slab(k, 3)
        c_copy(k, 2).wait_recv()
        add_slab(k, 2)
        lt[k, x, :, toks] = acc[...].T.astype(bf16)
        for d in (2, 1, 3):
            x_copy(k, d).start()
        d_copy(k, 0).start()

    def grad_slab(k, d):
        at = xt[(NX - d) % NX]
        part = jnp.dot(lt[k, at], gv[k], preferred_element_type=f32)
        gr[k, at] = part.astype(bf16).reshape(NZ, OWN, COLS)

        @pl.when(at != y)
        def _():
            d = lax.rem(at + NY - y, NY)
            for kind, some in ((Y_R0, pl.ds(0, NZ // 2)), (Y_R2, pl.ds(NZ // 2, NZ // 2))):
                src, dst = gr.at[k, at, some, :, low], rb0.at[k, d, some]
                copy(src, dst, ys.at[kind, k], yr.at[kind, k], (at * NZ + z, tensor)).start()

    def grad(k):
        if k == 0:
            load_g.wait()
        d_copy(k, 0).wait_recv()
        grad_slab(k, 0)
        x_copy(k, 1).wait_recv()
        d_copy(k, 1).start()
        x_copy(k, 3).wait_recv()
        d_copy(k, 3).start()
        d_copy(k, 1).wait_recv()
        grad_slab(k, 1)
        x_copy(k, 2).wait_recv()
        d_copy(k, 2).start()
        d_copy(k, 3).wait_recv()
        grad_slab(k, 3)
        d_copy(k, 2).wait_recv()
        grad_slab(k, 2)
        z_start(Z_R1, k)

    def reduce_second(k):
        z_arrive(Z_R1, k)
        total = gr[k, :, z, :, high].astype(f32)
        for d in range(1, NZ):
            total += rb1[k, d].astype(f32)
        s1[k] = total.astype(bf16)
        y_start(Y_R1, k)
        for kind, start in ((Y_R0, 0), (Y_R2, NZ // 2)):
            some = pl.ds(start, NZ // 2)
            y_arrive(kind, k)
            total = gr[k, y, some, :, low].astype(f32)
            for d in range(1, NY):
                total += rb0[k, d, some].astype(f32)
            s0[k, some] = total.astype(bf16)
            for to in range(start, start + NZ // 2):

                @pl.when(to != z)
                def _():
                    dst = q0.at[k, lax.rem(to + NZ - z, NZ)]
                    who = (y * NZ + to, tensor)
                    copy(s0.at[k, to], dst, zs.at[Z_R0, k], zr.at[Z_R0, k], who).start()

    def step(k, cols, grad_owned):
        first = beta_one * m1_ref[k, :, cols] + (1.0 - beta_one) * grad_owned
        second = beta_two * m2_ref[k, :, cols] + (1.0 - beta_two) * grad_owned * grad_owned
        nf_ref[k, :, cols] = first
        ns_ref[k, :, cols] = second
        low_step = first / bias_one / (jnp.sqrt(second / bias_two) + adam_eps)
        return low_step.astype(bf16)

    def moments(k):
        if k == 0:
            load_m1.wait()
            load_m2.wait()
        z_arrive(Z_R0, k)
        total = s0[k, z].astype(f32)
        for d in range(1, NZ):
            total += q0[k, d].astype(f32)
        low_step = step(k, low, total)
        for to in range(NY):
            lown[k, to] = low_step[:, to * LANES : (to + 1) * LANES]
        y_start(Y_L0, k)
        la[k, y, z] = lown[k, y]
        y_arrive(Y_R1, k)
        total = s1[k, y].astype(f32)
        for d in range(1, NY):
            total += q1[k, d].astype(f32)
        lb[k, y, z] = step(k, high, total)
        z_start(Z_L1, k)

    def rows_out(k):
        for d in (2, 1, 3):
            p_copy(k, d).start()
        p4[k, :, share, mine] = pg[k, :, z, share]

    def rows_in(k):
        p_all(k).wait_recv()
        e_copy(k).start()

    def spread_second(k):
        y_arrive(Y_L0, k)
        z_start(Z_L0, k)
        z_arrive(Z_L1, k)
        y_start(Y_L1, k)

    def update(k):
        e_copy(k).wait_recv()
        z_arrive(Z_L0, k)
        whole = jnp.dot(
            p4[k].reshape(NY * ROWS, NX * LANES),
            la[k].reshape(NX * LANES, LANES),
            preferred_element_type=f32,
        )
        uq[k] = whole.astype(bf16).reshape(NY, ROWS, LANES)
        y_start(Y_U, k)
        u_ref[k, :, pl.ds(pl.multiple_of(y * LANES, LANES), LANES)] = uq[k, y]

    def finish(k):
        y_arrive(Y_L1, k)
        part = jnp.dot(
            p_ref[k], lb[k].reshape(NX * LANES, LANES), preferred_element_type=f32
        )
        u_ref[k, :, high] = part.astype(bf16)
        y_arrive(Y_U, k)

    load_p.wait()
    pl.semaphore_wait(barrier, NZ - 1 + NY - 1 + NX - 1 + 1)

    for what, k in (
        (gather_first, 0), (gather_first, 1), (gather_second, 0), (gather_first, 2), (gather_second, 1),
        (lower, 0), (gather_second, 2), (lower, 1), (grad, 0), (lower, 2),
        (rows_out, 0), (rows_out, 1), (rows_out, 2),
        (grad, 1), (reduce_second, 0), (grad, 2), (moments, 0), (reduce_second, 1), (spread_second, 0),
        (rows_in, 0), (rows_in, 1), (moments, 1), (reduce_second, 2), (update, 0), (spread_second, 1),
        (rows_in, 2), (moments, 2), (update, 1), (spread_second, 2), (finish, 0), (update, 2), (finish, 1), (finish, 2),
    ):
        what(k)

    for k in range(NK):
        for kind in range(6):
            if kind != Z_P0 or k == NK - 1:
                z_all(kind, k).wait_send()
        for kind in range(8):
            y_all(kind, k).wait_send()
        for sent in (c_all, d_all, x_all, p_all, e_copy):
            sent(k).wait_send()


def on_device(activations, cotangent, projector, first_moment, second_moment):
    vmem = pl.BlockSpec(memory_space=pltpu.VMEM)
    hbm = pl.BlockSpec(memory_space=pltpu.HBM)
    dma = pltpu.SemaphoreType.DMA
    return pl.pallas_call(
        kernel,
        out_shape=(
            jax.ShapeDtypeStruct((NK, OWN, COLS), f32),
            jax.ShapeDtypeStruct((NK, OWN, COLS), f32),
            jax.ShapeDtypeStruct((NK, ROWS, COLS), bf16),
        ),
        in_specs=[hbm] * 5,
        out_specs=(vmem, vmem, vmem),
        scratch_shapes=[
            pltpu.VMEM((NK, ROWS, NX * LANES), bf16),
            pltpu.VMEM((NK, OWN, COLS), f32),
            pltpu.VMEM((NK, OWN, COLS), f32),
            pltpu.VMEM((NK, NY, NZ, ROWS, LANES), bf16),
            pltpu.VMEM((HALF, NY * SLAB), bf16),
            pltpu.VMEM((NK, TOK, COLS), bf16),
            pltpu.VMEM((HALF, LANES), f32),
            pltpu.VMEM((NK, NX, LANES, TOK), bf16),
            pltpu.VMEM((NK, NY, NZ, OWN, COLS), bf16),
            pltpu.VMEM((NK, NY, NZ, OWN, WIDE), bf16),
            pltpu.VMEM((NK, NZ, NY, OWN, COLS - WIDE), bf16),
            pltpu.VMEM((NK, NZ, OWN, WIDE), bf16),
            pltpu.VMEM((NK, NY, OWN, COLS - WIDE), bf16),
            pltpu.VMEM((NK, NZ, OWN, WIDE), bf16),
            pltpu.VMEM((NK, NY, OWN, COLS - WIDE), bf16),
            pltpu.VMEM((NK, NY, OWN, LANES), bf16),
            pltpu.VMEM((NK, NY, NZ, OWN, LANES), bf16),
            pltpu.VMEM((NK, NY, NZ, OWN, LANES), bf16),
            pltpu.VMEM((NK, NY, ROWS, NX * LANES), bf16),
            pltpu.VMEM((NK, NY, ROWS, LANES), bf16),
            dma((6, NK)), dma((6, NK)), dma((NK, NZ)),
            dma((8, NK)), dma((8, NK)), dma((NK, NY)),
            dma((NK,)), dma((NK, NY + 1)),
            dma((NK,)), dma((NK, NX)),
            dma((NK,)), dma((NK, NX)),
            dma((NK,)), dma((NK,)),
            dma((NK,)), dma((NK,)),
            dma((5,)),
        ],
        compiler_params=pltpu.CompilerParams(
            collective_id=0, has_side_effects=True, vmem_limit_bytes=52 * 2**20
        ),
        name="galore_step",
    )(projector, first_moment, second_moment, activations, cotangent)


def solution(mesh):
    placed = (
        P("dp", None),
        P(None, "dp", "tensor"),
        P(None, "dp", None),
        P(None, "dp", "tensor"),
        P(None, "dp", "tensor"),
    )
    return jax.shard_map(
        on_device,
        mesh=mesh,
        in_specs=placed,
        out_specs=(P(None, "dp", "tensor"), P(None, "dp", "tensor"), P(None, "dp", "tensor")),
        check_vma=False,
    )
```

time: 102 us -> 91.5 us (0.90)
  Pallas kernels: 93.6 us -> 85.7 us
  local copies, waits for them, and re-layouts: 6.78 us -> 4.95 us
    pallas_call x1, Pallas kernels: 93.6 us -> 85.7 us  [on_device(): pl.pallas_call(kernel, out_shape=(jax.ShapeDtypeStruct((NK, OWN, COLS), f...]
    unnamed x11 -> x9, local copies, waits for them, and re-layouts: 6.78 us -> 4.95 us
where the time goes in v3:
time: 91.5 us; the launch traced here: 91.3 us
  Pallas kernels  85.7 us (94%)
  local copies, waits for them, and re-layouts  4.95 us (5%)
    pallas_call x1, Pallas kernels, on_device(): pl.pallas_call(kernel, out_shape=(jax.ShapeDtypeStruct((NK, OWN, COLS), f...  85.7 us
    unnamed x9, local copies, waits for them, and re-layouts  4.95 us

profile of v3, /device:TPU:2, one launch (start us, length us, event | category | flops | bytes accessed | tf_op | source)
XLA Modules:
  0.0 91.3 jit_solution(7349853984886414452)
XLA Ops:
  0.6 0.0 copy-start
  0.6 1.0 %copy-done = bf16[3,160,512]{2,1,0:T(8,128)(2,1)S(1)} copy-done((bf16[3,160,512]{2,1,0:T(8,128)(2,1)S(1)}, bf16[3,160,512]{2,1,0:T(8,128)(2,1)}, u32[]{:S(2)}) %copy-start) | copy-done | bytes 491544
  1.7 0.0 copy-start.1
  1.7 0.9 copy-done.1
  2.6 0.0 copy-start.2
  2.6 0.9 copy-done.2
  3.5 85.7 %galore_step.1 = (f32[3,16,640]{2,1,0:T(8,128)S(1)}, f32[3,16,640]{2,1,0:T(8,128)S(1)}, bf16[3,160,640]{2,1,0:T(8,128)(2,1)S(1)}) custom-call(bf16[3,160,512]{2,1,0:T(8,128)(2,1)S(1)} %copy-done, f32[3,16,640]{2,1,0:T(8,128)S(1)} %copy-done.1, f32[3,16,640]{2,1,0:T(8,128)S(1)} %copy-done.2, bf16[768,5120]{1,0:T(8,128)(2,1)} %a_hbm.1, bf16[3,768,640]{2,1,0:T(8,128)(2,1)} %g_hbm.1), custom_call_target="tpu_custom_call" | custom-call | tf_op jit(solution)/shard_map/galore_step/pallas_call | solution.py:394
  89.2 0.7 copy.11
  89.9 0.6 copy.12
  90.5 0.8 copy.13
Async XLA Ops:
  0.6 1.0 %copy-start = (bf16[3,160,512]{2,1,0:T(8,128)(2,1)S(1)}, bf16[3,160,512]{2,1,0:T(8,128)(2,1)}, u32[]{:S(2)}) copy-start(bf16[3,160,512]{2,1,0:T(8,128)(2,1)} %p_hbm.1) | copy-start | bytes 1474564
  1.7 0.9 copy-start.1
  2.6 0.9 copy-start.2

commit v4 on v3

--- a/solution.py
+++ b/solution.py
@@ -87,7 +87,7 @@
     def z_copy(kind, k, d):
         to = zt[d]
         if kind == Z_P0:
-            src, dst = p_ref.at[k, rows0, mine], pg.at[k, y, z, rows0]
+            src, dst = p_hbm.at[k, rows0, mine], pg.at[k, y, z, rows0]
         elif kind == Z_P1:
             src = dst = pg.at[k, :, z, rows1]
         elif kind == Z_R1:
@@ -102,7 +102,7 @@
     def y_copy(kind, k, d):
         to = yt[d]
         if kind == Y_P1:
-            src, dst = p_ref.at[k, rows1, mine], pg.at[k, y, z, rows1]
+            src, dst = p_hbm.at[k, rows1, mine], pg.at[k, y, z, rows1]
         elif kind == Y_R1:
             src, dst = s1.at[k, to], q1.at[k, d]
         elif kind == Y_L0:
@@ -203,6 +203,8 @@
             z_all(Z_P0, k - 1).wait_send()
         z_start(Z_P0, k)
         y_start(Y_P1, k)
+        if k == 0:
+            load_p.wait()
         pg[k, y, z, share] = p_ref[k, share, mine]
         y_block(k, z)
 
@@ -228,17 +230,17 @@
         c_copy(k, NY).start()
         if k == 0:
             load_a.wait()
-        c_copy(k, NY).wait_recv()
-        c_copy(k, 0).wait_recv()
-        add_slab(k, 0, True)
         y_slab(k, 1).wait_recv()
         c_copy(k, 1).start()
         y_slab(k, 3).wait_recv()
         c_copy(k, 3).start()
+        y_slab(k, 2).wait_recv()
+        c_copy(k, 2).start()
+        c_copy(k, NY).wait_recv()
+        c_copy(k, 0).wait_recv()
+        add_slab(k, 0, True)
         c_copy(k, 1).wait_recv()
         add_slab(k, 1)
-        y_slab(k, 2).wait_recv()
-        c_copy(k, 2).start()
         c_copy(k, 3).wait_recv()
         add_slab(k, 3)
         c_copy(k, 2).wait_recv()
@@ -364,16 +366,16 @@
         u_ref[k, :, high] = part.astype(bf16)
         y_arrive(Y_U, k)
 
-    load_p.wait()
     pl.semaphore_wait(barrier, NZ - 1 + NY - 1 + NX - 1 + 1)
 
     for what, k in (
         (gather_first, 0), (gather_first, 1), (gather_second, 0), (gather_first, 2), (gather_second, 1),
         (lower, 0), (gather_second, 2), (lower, 1), (grad, 0), (lower, 2),
-        (rows_out, 0), (rows_out, 1), (rows_out, 2),
-        (grad, 1), (reduce_second, 0), (grad, 2), (moments, 0), (reduce_second, 1), (spread_second, 0),
-        (rows_in, 0), (rows_in, 1), (moments, 1), (reduce_second, 2), (update, 0), (spread_second, 1),
-        (rows_in, 2), (moments, 2), (update, 1), (spread_second, 2), (finish, 0), (update, 2), (finish, 1), (finish, 2),
+        (grad, 1), (reduce_second, 0), (grad, 2), (rows_out, 0), (rows_out, 1),
+        (rows_out, 2), (moments, 0), (reduce_second, 1), (spread_second, 0), (moments, 1),
+        (rows_in, 0), (rows_in, 1), (reduce_second, 2), (spread_second, 1), (update, 0),
+        (rows_in, 2), (moments, 2), (update, 1), (spread_second, 2), (update, 2),
+        (finish, 0), (finish, 1), (finish, 2),
     ):
         what(k)
 
@@ -387,17 +389,29 @@
             sent(k).wait_send()
 
 
+def place(nf, ns, u, nf_out, ns_out, u_out, sem):
+    copies = [
+        pltpu.make_async_copy(src, dst, sem.at[i])
+        for i, (src, dst) in enumerate(((u, u_out), (nf, nf_out), (ns, ns_out)))
+    ]
+    for one in copies:
+        one.start()
+    for one in copies:
+        one.wait()
+
+
 def on_device(activations, cotangent, projector, first_moment, second_moment):
     vmem = pl.BlockSpec(memory_space=pltpu.VMEM)
     hbm = pl.BlockSpec(memory_space=pltpu.HBM)
     dma = pltpu.SemaphoreType.DMA
-    return pl.pallas_call(
+    shapes = (
+        jax.ShapeDtypeStruct((NK, OWN, COLS), f32),
+        jax.ShapeDtypeStruct((NK, OWN, COLS), f32),
+        jax.ShapeDtypeStruct((NK, ROWS, COLS), bf16),
+    )
+    results = pl.pallas_call(
         kernel,
-        out_shape=(
-            jax.ShapeDtypeStruct((NK, OWN, COLS), f32),
-            jax.ShapeDtypeStruct((NK, OWN, COLS), f32),
-            jax.ShapeDtypeStruct((NK, ROWS, COLS), bf16),
-        ),
+        out_shape=shapes,
         in_specs=[hbm] * 5,
         out_specs=(vmem, vmem, vmem),
         scratch_shapes=[
@@ -435,6 +449,15 @@
         ),
         name="galore_step",
     )(projector, first_moment, second_moment, activations, cotangent)
+    return pl.pallas_call(
+        place,
+        out_shape=shapes,
+        in_specs=[pl.BlockSpec(memory_space=pl.ANY)] * 3,
+        out_specs=(hbm,) * 3,
+        scratch_shapes=[dma((3,))],
+        compiler_params=pltpu.CompilerParams(vmem_limit_bytes=16 * 2**20),
+        name="place_results",
+    )(*results)
 
 
 def solution(mesh):

time: 91.5 us -> 85.1 us (0.930)
  Pallas kernels: 85.7 us -> 81.1 us
  local copies, waits for them, and re-layouts: 4.95 us -> 2.83 us
    pallas_call x1 -> x2, Pallas kernels: 85.7 us -> 81.1 us  [the longest x1 80.2 us: on_device(): pl.pallas_call(kernel, out_shape=shapes, in_specs=[hbm] * 5, out_specs=(v...]
    unnamed x9 -> x6, local copies, waits for them, and re-layouts: 4.95 us -> 2.83 us
where the time goes in v4:
time: 85.1 us; the launch traced here: 84.6 us
  Pallas kernels  81.1 us (95%)
  local copies, waits for them, and re-layouts  2.83 us (3%)
    pallas_call x1, Pallas kernels, on_device(): pl.pallas_call(kernel, out_shape=shapes, in_specs=[hbm] * 5, out_specs=(v...  80.2 us
    unnamed x6, local copies, waits for them, and re-layouts  2.83 us

profile of v4, /device:TPU:2, one launch (start us, length us, event | category | flops | bytes accessed | tf_op | source)
XLA Modules:
  0.0 84.6 jit_solution(14330931417230401110)
XLA Ops:
  0.6 0.0 copy-start
  0.6 1.0 %copy-done = bf16[3,160,512]{2,1,0:T(8,128)(2,1)S(1)} copy-done((bf16[3,160,512]{2,1,0:T(8,128)(2,1)S(1)}, bf16[3,160,512]{2,1,0:T(8,128)(2,1)}, u32[]{:S(2)}) %copy-start) | copy-done | bytes 491544
  1.7 0.0 copy-start.1
  1.7 0.9 %copy-done.1 = f32[3,16,640]{2,1,0:T(8,128)S(1)} copy-done((f32[3,16,640]{2,1,0:T(8,128)S(1)}, f32[3,16,640]{2,1,0:T(8,128)}, u32[]{:S(2)}) %copy-start.1) | copy-done | bytes 122904
  2.6 0.0 copy-start.2
  2.6 0.9 %copy-done.2 = f32[3,16,640]{2,1,0:T(8,128)S(1)} copy-done((f32[3,16,640]{2,1,0:T(8,128)S(1)}, f32[3,16,640]{2,1,0:T(8,128)}, u32[]{:S(2)}) %copy-start.2) | copy-done | bytes 122904
  3.5 80.2 %galore_step.1 = (f32[3,16,640]{2,1,0:T(8,128)S(1)}, f32[3,16,640]{2,1,0:T(8,128)S(1)}, bf16[3,160,640]{2,1,0:T(8,128)(2,1)S(1)}) custom-call(bf16[3,160,512]{2,1,0:T(8,128)(2,1)S(1)} %copy-done, f32[3,16,640]{2,1,0:T(8,128)S(1)} %copy-done.1, f32[3,16,640]{2,1,0:T(8,128)S(1)} %copy-done.2, bf16[768,5120]{1,0:T(8,128)(2,1)} %a_hbm.1, bf16[3,768,640]{2,1,0:T(8,128)(2,1)} %g_hbm.1), custom_call_target="tpu_custom_call" | custom-call | tf_op jit(solution)/shard_map/galore_step/pallas_call | solution.py:412
  83.7 0.9 %place_results.1 = (f32[3,16,640]{2,1,0:T(8,128)}, f32[3,16,640]{2,1,0:T(8,128)}, bf16[3,160,640]{2,1,0:T(8,128)(2,1)}) custom-call(f32[3,16,640]{2,1,0:T(8,128)S(1)} %get-tuple-element.6.nf, f32[3,16,640]{2,1,0:T(8,128)S(1)} %get-tuple-element.7.ns, bf16[3,160,640]{2,1,0:T(8,128)(2,1)S(1)} %get-tuple-element.8.u), custom_call_target="tpu_custom_call" | custom-call | tf_op jit(solution)/shard_map/place_results/pallas_call | solution.py:452
Async XLA Ops:
  0.6 1.0 %copy-start = (bf16[3,160,512]{2,1,0:T(8,128)(2,1)S(1)}, bf16[3,160,512]{2,1,0:T(8,128)(2,1)}, u32[]{:S(2)}) copy-start(bf16[3,160,512]{2,1,0:T(8,128)(2,1)} %p_hbm.1) | copy-start | bytes 1474564
  1.7 0.9 %copy-start.1 = (f32[3,16,640]{2,1,0:T(8,128)S(1)}, f32[3,16,640]{2,1,0:T(8,128)}, u32[]{:S(2)}) copy-start(f32[3,16,640]{2,1,0:T(8,128)} %m1_hbm.1) | copy-start | bytes 368644
  2.6 0.9 %copy-start.2 = (f32[3,16,640]{2,1,0:T(8,128)S(1)}, f32[3,16,640]{2,1,0:T(8,128)}, u32[]{:S(2)}) copy-start(f32[3,16,640]{2,1,0:T(8,128)} %m2_hbm.1) | copy-start | bytes 368644

commit v5 on v4

--- a/solution.py
+++ b/solution.py
@@ -265,20 +265,12 @@
     def grad(k):
         if k == 0:
             load_g.wait()
-        d_copy(k, 0).wait_recv()
-        grad_slab(k, 0)
-        x_copy(k, 1).wait_recv()
-        d_copy(k, 1).start()
-        x_copy(k, 3).wait_recv()
-        d_copy(k, 3).start()
-        d_copy(k, 1).wait_recv()
-        grad_slab(k, 1)
-        x_copy(k, 2).wait_recv()
-        d_copy(k, 2).start()
-        d_copy(k, 3).wait_recv()
-        grad_slab(k, 3)
-        d_copy(k, 2).wait_recv()
-        grad_slab(k, 2)
+        for d in (1, 3, 2):
+            x_copy(k, d).wait_recv()
+            d_copy(k, d).start()
+        for d in (0, 1, 3, 2):
+            d_copy(k, d).wait_recv()
+            grad_slab(k, d)
         z_start(Z_R1, k)
 
     def reduce_second(k):

time: 85.1 us -> 84.7 us (level)
  no operation moved by 1% of the time
where the time goes in v5:
time: 84.7 us; the launch traced here: 84.5 us
  Pallas kernels  81.1 us (96%)
  local copies, waits for them, and re-layouts  2.83 us (3%)
    pallas_call x1, Pallas kernels, on_device(): pl.pallas_call(kernel, out_shape=shapes, in_specs=[hbm] * 5, out_specs=(v...  80.1 us
    unnamed x6, local copies, waits for them, and re-layouts  2.83 us

profile of v5, /device:TPU:2, one launch (start us, length us, event | category | flops | bytes accessed | tf_op | source)
XLA Modules:
  0.0 84.5 jit_solution(10918550142623932652)
XLA Ops:
  0.6 0.0 copy-start
  0.6 1.0 %copy-done = bf16[3,160,512]{2,1,0:T(8,128)(2,1)S(1)} copy-done((bf16[3,160,512]{2,1,0:T(8,128)(2,1)S(1)}, bf16[3,160,512]{2,1,0:T(8,128)(2,1)}, u32[]{:S(2)}) %copy-start) | copy-done | bytes 491544
  1.7 0.0 copy-start.1
  1.7 0.9 %copy-done.1 = f32[3,16,640]{2,1,0:T(8,128)S(1)} copy-done((f32[3,16,640]{2,1,0:T(8,128)S(1)}, f32[3,16,640]{2,1,0:T(8,128)}, u32[]{:S(2)}) %copy-start.1) | copy-done | bytes 122904
  2.6 0.0 copy-start.2
  2.6 0.9 %copy-done.2 = f32[3,16,640]{2,1,0:T(8,128)S(1)} copy-done((f32[3,16,640]{2,1,0:T(8,128)S(1)}, f32[3,16,640]{2,1,0:T(8,128)}, u32[]{:S(2)}) %copy-start.2) | copy-done | bytes 122904
  3.5 80.1 %galore_step.1 = (f32[3,16,640]{2,1,0:T(8,128)S(1)}, f32[3,16,640]{2,1,0:T(8,128)S(1)}, bf16[3,160,640]{2,1,0:T(8,128)(2,1)S(1)}) custom-call(bf16[3,160,512]{2,1,0:T(8,128)(2,1)S(1)} %copy-done, f32[3,16,640]{2,1,0:T(8,128)S(1)} %copy-done.1, f32[3,16,640]{2,1,0:T(8,128)S(1)} %copy-done.2, bf16[768,5120]{1,0:T(8,128)(2,1)} %a_hbm.1, bf16[3,768,640]{2,1,0:T(8,128)(2,1)} %g_hbm.1), custom_call_target="tpu_custom_call" | custom-call | tf_op jit(solution)/shard_map/galore_step/pallas_call | solution.py:404
  83.6 0.9 %place_results.1 = (f32[3,16,640]{2,1,0:T(8,128)}, f32[3,16,640]{2,1,0:T(8,128)}, bf16[3,160,640]{2,1,0:T(8,128)(2,1)}) custom-call(f32[3,16,640]{2,1,0:T(8,128)S(1)} %get-tuple-element.6.nf, f32[3,16,640]{2,1,0:T(8,128)S(1)} %get-tuple-element.7.ns, bf16[3,160,640]{2,1,0:T(8,128)(2,1)S(1)} %get-tuple-element.8.u), custom_call_target="tpu_custom_call" | custom-call | tf_op jit(solution)/shard_map/place_results/pallas_call | solution.py:444
Async XLA Ops:
  0.6 1.0 %copy-start = (bf16[3,160,512]{2,1,0:T(8,128)(2,1)S(1)}, bf16[3,160,512]{2,1,0:T(8,128)(2,1)}, u32[]{:S(2)}) copy-start(bf16[3,160,512]{2,1,0:T(8,128)(2,1)} %p_hbm.1) | copy-start | bytes 1474564
  1.7 0.9 %copy-start.1 = (f32[3,16,640]{2,1,0:T(8,128)S(1)}, f32[3,16,640]{2,1,0:T(8,128)}, u32[]{:S(2)}) copy-start(f32[3,16,640]{2,1,0:T(8,128)} %m1_hbm.1) | copy-start | bytes 368644
  2.6 0.9 %copy-start.2 = (f32[3,16,640]{2,1,0:T(8,128)S(1)}, f32[3,16,640]{2,1,0:T(8,128)}, u32[]{:S(2)}) copy-start(f32[3,16,640]{2,1,0:T(8,128)} %m2_hbm.1) | copy-start | bytes 368644
